TPU v7x, 128 devices: a whole 4x4x4 slice. The times are simulated.
128 devices in a mesh: seq: 8 (over x_hi, z), doc: 16 (over x_lo, y, core).
Axes of the slice: x: 4 (x_hi: 2, x_lo: 2; x = x_hi * 2 + x_lo), y: 4, z: 4, core: 2. Of those that a mesh axis runs over, the one named last changes fastest.
Arguments:
- hidden_in: bfloat16 [16, 1024, 2880], P('doc', 'seq'), may hold values from -6 to 6
- queries: bfloat16 [16, 1024, 4096], P('doc', 'seq'), may hold values from -8 to 8
- key_heads: bfloat16 [16, 1024, 512], P('doc', 'seq'), may hold values from -8 to 8
- values: bfloat16 [16, 1024, 512], P('doc', 'seq'), may hold values from -6 to 6
- doc_lengths: int32 [16], P('doc'), may hold values from 1 to 1024, 10240 in all
- out_weight: bfloat16 [4096, 2880], P('seq'), may hold values from -0.75 to 0.75
- norm_gain: bfloat16 [2880], replicated, may hold values from 0.099609375 to 1.8984375
- router_weight: bfloat16 [2880, 64], replicated, may hold values from -0.109375 to 0.109375
- expert_ids: int32 [16, 1024, 4], P('doc', 'seq'), may hold values from 0 to 63, all different within a row; in each aligned block of 128 rows (0 to 127, 128 to 255, ..., all dimensions but the last counted through in order) at most 12 rows name the same one
- gate_weight: bfloat16 [128, 2880, 768], P(('seq', 'doc')), may hold values from -0.109375 to 0.109375
- up_weight: bfloat16 [128, 2880, 768], P(('seq', 'doc')), may hold values from -0.109375 to 0.109375
- down_weight: bfloat16 [128, 768, 2880], P(('seq', 'doc')), may hold values from -0.15625 to 0.15625
Outputs:
- layer_out: bfloat16 [16, 1024, 2880], P('doc', 'seq')
Inputs may be any that keep to these rules, and one draw needn't show every extreme that they name: `doc_lengths`: the lengths sum to 10240, and the longest is 1024. `expert_ids`: each token names 4 different experts. Among the 128 positions that one device holds (aligned blocks of a document), no expert is named more than 12 times, and in some such block an expert is named exactly 12 times.
All inputs are finite; a program needn't handle non-finite values. No bound on the sum of `doc_lengths` on one device may be relied on, other than what follows from the above.
Results may differ from a plain program's by a relative error of at most 0.02.
Values may be sent and summed in bfloat16 or wider, within the bound.
No kernel may reach another device: no remote copies, remote signals or barrier semaphores. Data moves between devices by JAX's collectives and lax.ppermute only.
A program may use at most 128 MiB of HBM per device.

v0:
```python
import jax
import jax.numpy as jnp
from jax import lax
from jax.sharding import PartitionSpec as P

HEADS = 64
KVH = 8
HD = 64
TOP = 4
negative_fill = -1e30
swiglu_alpha = 1.702
norm_eps = 1e-05


def rounded(tensor_in):
    return lax.optimization_barrier(tensor_in.astype(jnp.bfloat16))


def local(
    hidden_in,
    queries,
    key_heads,
    values,
    doc_lengths,
    out_weight,
    norm_gain,
    router_weight,
    expert_ids,
    gate_weight,
    up_weight,
    down_weight,
):
    tokens_dev = hidden_in.shape[1]
    model_width = hidden_in.shape[2]
    doc_length = doc_lengths[0]
    group_size = HEADS // KVH
    score_scale = HD ** (-0.5)
    own_queries = queries[0].reshape(tokens_dev, KVH, group_size, HD)
    query_pos = lax.axis_index("seq") * tokens_dev + jnp.arange(tokens_dev, dtype=jnp.int32)
    run_top = jnp.full((KVH, group_size, tokens_dev), negative_fill, jnp.float32)
    piece_keys = lax.all_gather(key_heads, "seq", axis=1, tiled=True)
    piece_values = lax.all_gather(values, "seq", axis=1, tiled=True)
    piece_rows = piece_keys.shape[1]
    key_block = piece_keys[0].reshape(piece_rows, KVH, HD)
    value_block = piece_values[0].reshape(piece_rows, KVH, HD)
    key_pos = jnp.arange(piece_rows, dtype=jnp.int32)
    allowed = (key_pos[None, :] <= query_pos[:, None]) & (key_pos[None, :] < doc_length)
    scores = (
        jnp.einsum("qkgd,jkd->kgqj", own_queries, key_block, preferred_element_type=jnp.float32)
        * score_scale
    )
    scores = jnp.where(allowed, scores, negative_fill)
    new_top = jnp.maximum(run_top, jnp.max(scores, axis=-1))
    weights = jnp.where(allowed, jnp.exp(scores - new_top[..., None]), 0.0)
    new_total = jnp.sum(weights, axis=-1)
    update = jnp.einsum(
        "kgqj,jkd->kgqd",
        weights.astype(jnp.bfloat16),
        value_block,
        preferred_element_type=jnp.float32,
    )
    own_out = (update / new_total[..., None]).astype(jnp.bfloat16)
    own_out = own_out.transpose(2, 0, 1, 3).reshape(1, tokens_dev, HEADS * HD)
    attended = lax.all_to_all(own_out, "seq", split_axis=2, concat_axis=1, tiled=True)[0]
    attention_sum = lax.psum_scatter(
        jnp.dot(attended, out_weight, preferred_element_type=jnp.float32).astype(jnp.bfloat16),
        "seq",
        scatter_dimension=0,
        tiled=True,
    ).astype(jnp.float32)
    residual = rounded(hidden_in[0].astype(jnp.float32) + attention_sum).astype(jnp.float32)
    mean_square = jnp.mean(residual * residual, axis=-1, keepdims=True)
    normed = (residual * lax.rsqrt(mean_square + norm_eps) * norm_gain.astype(jnp.float32)).astype(
        jnp.bfloat16
    )
    logits = jnp.dot(normed, router_weight, preferred_element_type=jnp.float32)
    expert_count = router_weight.shape[1]
    chosen_ids = expert_ids[0]
    expert_range = jnp.arange(expert_count, dtype=jnp.int32)
    matches = chosen_ids[:, :, None] == expert_range[None, None, :]
    chosen_logits = jnp.sum(jnp.where(matches, logits[:, None, :], 0.0), axis=-1)
    raised = jnp.exp(chosen_logits)
    route_share = raised / jnp.sum(raised, axis=-1, keepdims=True)
    capacity = 2 * (tokens_dev * TOP * 3 // (4 * expert_count))
    flat_ids = chosen_ids.reshape(-1)
    one_hot = (flat_ids[:, None] == expert_range[None, :]).astype(jnp.int32)
    slot_rank = jnp.sum(jnp.cumsum(one_hot, axis=0) * one_hot, axis=1) - 1
    dest_row = flat_ids * capacity + slot_rank
    pair_count = tokens_dev * TOP
    slot_table = (
        jnp.full((expert_count * capacity,), tokens_dev, jnp.int32)
        .at[dest_row]
        .set(jnp.arange(pair_count, dtype=jnp.int32) // TOP)
    )
    padded = jnp.concatenate([normed, jnp.zeros((1, model_width), jnp.bfloat16)], axis=0)
    outgoing = padded[slot_table].reshape(expert_count, capacity, model_width)
    doubled = jnp.broadcast_to(outgoing[:, None], (expert_count, 2, capacity, model_width)).reshape(
        2 * expert_count, capacity, model_width
    )
    arrived = lax.all_to_all(doubled, ("seq", "doc"), split_axis=0, concat_axis=0, tiled=True)
    flat_rows = arrived.reshape(-1, model_width)
    gate_val = jnp.dot(flat_rows, gate_weight[0], preferred_element_type=jnp.float32)
    up_val = jnp.dot(flat_rows, up_weight[0], preferred_element_type=jnp.float32)
    active = (gate_val * jax.nn.sigmoid(swiglu_alpha * gate_val) * (up_val + 1.0)).astype(
        jnp.bfloat16
    )
    arrived_back = lax.all_to_all(
        jnp.dot(active, down_weight[0], preferred_element_type=jnp.float32)
        .astype(jnp.bfloat16)
        .reshape(arrived.shape),
        ("seq", "doc"),
        split_axis=0,
        concat_axis=0,
        tiled=True,
    )
    arrived_back = arrived_back.reshape(expert_count, 2, capacity, model_width)
    expert_out = rounded(
        arrived_back[:, 0].astype(jnp.float32) + arrived_back[:, 1].astype(jnp.float32)
    )
    expert_out = expert_out.reshape(expert_count * capacity, model_width)
    gathered = expert_out[dest_row].reshape(tokens_dev, TOP, model_width)
    mixture_sum = jnp.einsum("tk,tkd->td", route_share, gathered.astype(jnp.float32))
    layer_out = (residual + mixture_sum).astype(jnp.bfloat16)
    return layer_out[None]


def solution(mesh):
    in_specs = (
        P("doc", "seq", None),
        P("doc", "seq", None),
        P("doc", "seq", None),
        P("doc", "seq", None),
        P("doc"),
        P("seq", None),
        P(),
        P(),
        P("doc", "seq", None),
        P(("seq", "doc"), None, None),
        P(("seq", "doc"), None, None),
        P(("seq", "doc"), None, None),
    )
    out_specs = P("doc", "seq", None)
    return jax.shard_map(local, mesh=mesh, in_specs=in_specs, out_specs=out_specs, check_vma=False)
```

profile of v0, /device:TPU:32, one launch (start us, length us, event | category | flops | bytes accessed | tf_op | source)
XLA Modules:
  0.0 778.7 jit_solution(9515316538338982292)
XLA Ops:
  6.5 0.7 all-gather.3.cloned.1.call-update
  7.3 0.7 all-gather.5.cloned.1.call-update
  8.7 2.3 copy.71
  11.2 46.7 %all-gather.3.cloned.1.call-done = bf16[1,1024,512]{2,1,0:T(8,128)(2,1)} async-done(((bf16[1,128,512]{2,1,0:T(8,128)(2,1)}), bf16[1,1024,512]{2,1,0:T(8,128)(2,1)}) %all-gather.3.cloned.1.call-update) | async-done | bytes 1048592 | tf_op jit(solution)/shard_map/all_gather | solution.py:41
  57.9 2.3 copy.70
  60.1 14.7 %fusion = (f32[8,8,128]{2,1,0:T(8,128)S(1)}, f32[8,1024,128,8]{2,1,3,0:T(8,128)}) fusion(pred[128,1024]{0,1:T(8,128)(4,1)S(1)} %fusion.27, bf16[1024,8,64,1]{0,2,3,1:T(8,128)(2,1)} %bitcast.110, bf16[128,8,8,64]{0,3,2,1:T(8,128)(2,1)} %bitcast.109), kind=kOutput, calls=%fused_computation.5 | convolution fusion | flops 1098899456 | bytes 35815424 | tf_op jit(solution)/shard_map/qkgd,jkd->kgqj/dot_general | solution.py:49
  74.8 14.9 %fusion.1 = f32[8,8,128]{2,1,0:T(8,128)S(1)} fusion(f32[8,1024,128,8]{2,1,3,0:T(8,128)} %get-tuple-element.6, f32[8,8,128]{2,1,0:T(8,128)S(1)} %broadcast_maximum_fusion, pred[128,1024]{0,1:T(8,128)(4,1)S(1)} %fusion.27), kind=kLoop, calls=%fused_computation.6 | loop fusion | flops 41934848 | bytes 33751040 | tf_op jit(solution)/shard_map/reduce_sum | solution.py:55
  89.7 15.7 %all-gather.5.cloned.1.call-done = bf16[1,1024,512]{2,1,0:T(8,128)(2,1)} async-done(((bf16[1,128,512]{2,1,0:T(8,128)(2,1)}), bf16[1,1024,512]{2,1,0:T(8,128)(2,1)}) %all-gather.5.cloned.1.call-update) | async-done | bytes 1048592 | tf_op jit(solution)/shard_map/all_gather | solution.py:42
  105.5 2.3 copy.72
  107.7 14.5 %fusion.18 = bf16[128,8,8,64]{0,3,2,1:T(8,128)(2,1)S(1)} fusion(bf16[1024,8,64,1]{0,2,3,1:T(8,128)(2,1)} %bitcast.113, f32[8,1024,128,8]{2,1,3,0:T(8,128)} %get-tuple-element.6, f32[8,8,128]{2,1,0:T(8,128)S(1)} %broadcast_maximum_fusion, pred[128,1024]{0,1:T(8,128)(4,1)S(1)} %fusion.27, f32[128,8,8]{0,2,1:T(8,128)S(1)} %bitcast.115), kind=kOutput, calls=%fused_computation.28 | convolution fusion | flops 1116733440 | bytes 35848192 | tf_op jit(solution)/shard_map/kgqj,jkd->kgqd/dot_general | solution.py:56
  122.2 17.3 %copy.101 = bf16[1,128,4096]{1,0,2:T(2,128)(2,1)} copy(bf16[1,128,4096]{1,2,0:T(8,128)(2,1)S(1)} %bitcast.112) | data formatting | bytes 2097152 | tf_op jit(solution)/shard_map/reshape | solution.py:63
  139.6 0.5 broadcast.127
  140.1 24.4 %reduce.2 = bf16[4096,128]{1,0:T(8,128)(2,1)} reduce(bf16[4096,1,128]{2,1,0:T(2,128)(2,1)} %bitcast.108, bf16[]{:T(256)} %broadcast.127), dimensions={1}, to_apply=%bitcast.104.reduce_sub_computation | reduce | bytes 2097154
  164.5 2.2 reshape.147
  166.7 19.9 %all_to_all.25 = bf16[8,2,32768]{2,1,0:T(2,128)(2,1)} all-to-all(bf16[8,2,32768]{2,1,0:T(2,128)(2,1)} %reshape.147), channel_id=1, replica_groups=mesh['seq'=8,'doc'=16] {'seq'}, dimensions={0} | all-to-all | bytes 2097152 | tf_op jit(solution)/shard_map/all_to_all | solution.py:64
  186.6 5.8 reshape.148
  192.4 2.7 copy.92
  195.1 2.3 copy.75
  197.4 6.3 convolution_convert_fusion.1
  203.7 8.5 %copy.90 = bf16[1024,2880]{1,0:T(8,128)(2,1)} copy(bf16[1024,2880]{0,1:T(8,128)(2,1)} %convolution_convert_fusion.1) | data formatting | bytes 11796480
  212.2 0.7 copy-done.6
  213.3 0.3 copy.69
  213.7 1.2 reduce-window.6
  215.6 2.4 scatter_custom_fusion
  218.0 88.8 %reduce-scatter.4.cloned.1.call-done = bf16[128,2880]{1,0:T(8,128)(2,1)} async-done(((bf16[1024,2880]{1,0:T(8,128)(2,1)}), bf16[128,2880]{1,0:T(8,128)(2,1)}) %reduce-scatter.4.cloned.1.call-update) | async-done | bytes 737296 | tf_op jit(solution)/shard_map/reduce_scatter | solution.py:65
  306.8 1.3 fusion.25
  308.1 0.2 fusion.21
  308.4 0.6 copy-done.2
  309.0 0.2 fusion.23
  309.3 4.8 gather_fusion
  314.2 7.3 broadcast_in_dim.65
  321.5 4.5 broadcast_in_dim.66
  326.0 143.3 %all_to_all.26 = bf16[128,12,2880]{2,1,0:T(8,128)(2,1)} all-to-all(bf16[128,12,2880]{2,1,0:T(8,128)(2,1)S(1)} %bitcast.106), channel_id=1, replica_groups=mesh['seq'=8,'doc'=16] {'seq','doc'}, dimensions={0} | all-to-all | bytes 17694720 | tf_op jit(solution)/shard_map/all_to_all | solution.py:100
  469.3 14.6 %reshape.107 = bf16[1536,2880]{1,0:T(8,128)(2,1)} reshape(bf16[128,12,2880]{2,1,0:T(8,128)(2,1)} %all_to_all.26) | data formatting | bytes 17694720 | tf_op jit(solution)/shard_map/reshape | solution.py:101
  483.9 12.7 %fusion.8 = f32[1536,768]{1,0:T(8,128)} fusion(bf16[1536,2880]{1,0:T(8,128)(2,1)} %reshape.107, bf16[1,2880,768]{2,1,0:T(8,128)(2,1)} %param.22), kind=kOutput, calls=%fused_computation.18 | convolution fusion | flops 6794772480 | bytes 17989632 | tf_op jit(solution)/shard_map/dot_general | solution.py:103
  496.6 23.8 %convolution_convert_fusion = bf16[1536,2880]{0,1:T(8,128)(2,1)} fusion(bf16[1,768,2880]{1,2,0:T(8,128)(2,1)} %param.23, f32[1536,768]{1,0:T(8,128)} %fusion.8, bf16[1536,2880]{1,0:T(8,128)(2,1)} %reshape.107, bf16[1,2880,768]{2,1,0:T(8,128)(2,1)} %param.21), kind=kOutput, calls=%fused_computation.11 | convolution fusion | flops 13603405824 | bytes 31260672 | tf_op jit(solution)/shard_map/dot_general | solution.py:108
  520.4 12.5 %copy.81 = bf16[1536,2880]{1,0:T(8,128)(2,1)} copy(bf16[1536,2880]{0,1:T(8,128)(2,1)} %convolution_convert_fusion) | data formatting | bytes 17694720 | tf_op jit(solution)/shard_map/convert_element_type | solution.py:109
  532.8 13.5 %reshape.108 = bf16[128,12,2880]{2,1,0:T(8,128)(2,1)} reshape(bf16[1536,2880]{1,0:T(8,128)(2,1)} %copy.81) | data formatting | bytes 17694720 | tf_op jit(solution)/shard_map/reshape | solution.py:110
  546.3 14.6 %all-to-all-start.2 = ((bf16[128,12,2880]{2,1,0:T(8,128)(2,1)}), bf16[128,12,2880]{2,1,0:T(8,128)(2,1)}, u32[]{:S(2)}, u32[]{:S(2)}) async-start(bf16[128,12,2880]{2,1,0:T(8,128)(2,1)} %reshape.108), calls=%async_computation.2 | async-start | bytes 24117248 | tf_op jit(solution)/shard_map/all_to_all | solution.py:107
  561.0 0.4 fusion.41
  561.6 171.4 %all-to-all-done.2 = bf16[128,12,2880]{2,1,0:T(8,128)(2,1)} async-done(((bf16[128,12,2880]{2,1,0:T(8,128)(2,1)}), bf16[128,12,2880]{2,1,0:T(8,128)(2,1)}, u32[]{:S(2)}, u32[]{:S(2)}) %all-to-all-start.2) | async-done | bytes 8847392 | tf_op jit(solution)/shard_map/all_to_all | solution.py:107
  733.0 8.5 %fusion.6 = bf16[64,12,2880]{2,1,0:T(8,128)(2,1)} fusion(bf16[64,2,12,2880]{3,2,1,0:T(8,128)(2,1)} %bitcast.24), kind=kLoop, calls=%fused_computation.12 | loop fusion | flops 8847360 | bytes 13271040 | tf_op jit(solution)/shard_map/convert_element_type | solution.py:16
  741.5 7.9 %reshape.110 = bf16[768,2880]{1,0:T(8,128)(2,1)} reshape(bf16[64,12,2880]{2,1,0:T(8,128)(2,1)} %fusion.6) | data formatting | bytes 8847360 | tf_op jit(solution)/shard_map/reshape | solution.py:120
  749.4 9.6 %gather_fusion.1 = bf16[512,2880]{1,0:T(8,128)(2,1)} fusion(bf16[768,2880]{1,0:T(8,128)(2,1)} %reshape.110, s32[1024]{0:T(1024)S(1)} %pad_clamp_fusion), kind=kCustom, calls=%fused_computation.1 | custom fusion | bytes 5900288 | tf_op jit(solution)/shard_map/gather | solution.py:121
  759.0 5.9 reshape.111
  764.9 3.7 fusion.42
  768.6 1.0 fusion.26
  769.6 2.3 copy.84
  (46 shorter events, 1.7 us)
Async XLA Ops:
  6.5 190.8 %copy-start = (bf16[512,2880]{0,1:T(8,128)(2,1)S(1)}, bf16[512,2880]{0,1:T(8,128)(2,1)}, u32[]{:S(2)}) copy-start(bf16[512,2880]{0,1:T(8,128)(2,1)} %param.17) | copy-start | bytes 8847364
  6.5 51.3 %all-gather.3.cloned.1.call-start = ((), (), s32[]{:S(2)}) async-start(), calls=%async_computation.4 | async-start | bytes 1179648 | tf_op jit(solution)/shard_map/all_gather | solution.py:41
  7.3 98.2 %all-gather.5.cloned.1.call-start = ((), (), s32[]{:S(2)}) async-start(), calls=%async_computation.5 | async-start | bytes 1179648 | tf_op jit(solution)/shard_map/all_gather | solution.py:42
  8.0 298.8 %reduce-scatter.4.cloned.1.call-start = ((), (), s32[]{:S(2)}) async-start(), calls=%async_computation.6 | async-start | bytes 6782976 | tf_op jit(solution)/shard_map/reduce_scatter | solution.py:65
  212.2 0.7 copy-start.6
  212.2 1.1 copy-start.4
  212.2 1.5 copy-start.7
  308.1 0.9 copy-start.2
  546.3 14.7 %copy-start.5 = (bf16[2880,64]{0,1:T(8,128)(2,1)S(1)}, bf16[2880,64]{0,1:T(8,128)(2,1)}, u32[]{:S(2)}) copy-start(bf16[2880,64]{0,1:T(8,128)(2,1)} %param.19) | copy-start | bytes 1105924
  546.3 186.7 %all-to-all-start.2 = ((bf16[128,12,2880]{2,1,0:T(8,128)(2,1)}), bf16[128,12,2880]{2,1,0:T(8,128)(2,1)}, u32[]{:S(2)}, u32[]{:S(2)}) async-start(bf16[128,12,2880]{2,1,0:T(8,128)(2,1)} %reshape.108), calls=%async_computation.2 | async-start | bytes 24117248 | tf_op jit(solution)/shard_map/all_to_all | solution.py:107
  759.0 12.9 %copy-start.1 = (bf16[512,2880]{0,1:T(8,128)(2,1)S(1)}, bf16[512,2880]{0,1:T(8,128)(2,1)}, u32[]{:S(2)}) copy-start(bf16[512,2880]{0,1:T(8,128)(2,1)} %param.17) | copy-start | bytes 8847364
  764.9 3.7 copy-start.3
Sparse Core Ops, SparseCore 0:
  9.7 48.1 all-gather.2
  60.2 45.1 all-gather.4
  212.3 94.4 reduce-scatter.3
where the time goes:
time: 787 us; the launch traced here: 779 us
  waiting for transfers between devices  324 us (41%)
  blocking collectives  163 us (21%)
  local copies, waits for them, and re-layouts  134 us (17%)
  matrix products  76 us (10%)
  other arithmetic  52.3 us (7%)
  starting transfers between devices  14.7 us (2%)
  between operations  14.2 us (2%)
    all_to_all x1, waiting for transfers between devices, local(): lax.all_to_all(jnp.dot(active, down_weight[0], preferred_element_type=jnp...  171 us
    all_to_all x1, blocking collectives, local(): lax.all_to_all(doubled, ('seq', 'doc'), split_axis=0, concat_axis=0, tile...  143 us
    reduce_scatter x1, waiting for transfers between devices, local(): lax.psum_scatter(jnp.dot(attended, out_weight, preferred_element_type=jnp...  88.8 us
    all_gather x1, waiting for transfers between devices, local(): piece_keys = lax.all_gather(key_heads, 'seq', axis=1, tiled=True)  46.7 us
    unnamed x1, other arithmetic  24.4 us
    unnamed x24, local copies, waits for them, and re-layouts  23.8 us
    dot_general x1, matrix products, local(): jnp.dot(active, down_weight[0], preferred_element_type=jnp.float32)  23.8 us
    all_to_all x1, blocking collectives, local(): lax.all_to_all(own_out, 'seq', split_axis=2, concat_axis=1, tiled=True)[0]  19.9 us
  transfers between devices with their start and end apart: 4, of which 4 were waited for; matrix products, arithmetic and copies ran while one was open for 5% of the time, Pallas kernels for 0%

commit v1 on v0

--- a/solution.py
+++ b/solution.py
@@ -61,7 +61,10 @@
     )
     own_out = (update / new_total[..., None]).astype(jnp.bfloat16)
     own_out = own_out.transpose(2, 0, 1, 3).reshape(1, tokens_dev, HEADS * HD)
-    attended = lax.all_to_all(own_out, "seq", split_axis=2, concat_axis=1, tiled=True)[0]
+    attended = jnp.concatenate(
+        lax.all_to_all(jnp.stack(jnp.split(own_out, lax.axis_size("seq"), axis=2)), "seq", 0, 0),
+        axis=1,
+    )[0]
     attention_sum = lax.psum_scatter(
         jnp.dot(attended, out_weight, preferred_element_type=jnp.float32).astype(jnp.bfloat16),
         "seq",

time: 787 us -> 738 us (0.938)
  other arithmetic: 52.3 us -> 27.8 us
  local copies, waits for them, and re-layouts: 134 us -> 122 us
  waiting for transfers between devices: 324 us -> 314 us
    unnamed x1 -> x0, other arithmetic: 24.4 us -> none
    reshape x1 -> x0, local copies, waits for them, and re-layouts: 17.3 us -> none  [local(): own_out = own_out.transpose(2, 0, 1, 3).reshape(1, tokens_dev, HEADS * HD)]
    all_to_all x1, waiting for transfers between devices: 171 us -> 161 us  [local(): lax.all_to_all(jnp.dot(active, down_weight[0], preferred_element_type=jnp...]
    unnamed x24 -> x35, local copies, waits for them, and re-layouts: 23.8 us -> 29.5 us
where the time goes in v1:
time: 738 us; the launch traced here: 728 us
  waiting for transfers between devices  314 us (43%)
  blocking collectives  162 us (22%)
  local copies, waits for them, and re-layouts  122 us (17%)
  matrix products  74.8 us (10%)
  other arithmetic  27.8 us (4%)
  starting transfers between devices  14 us (2%)
  between operations  14 us (2%)
    all_to_all x1, waiting for transfers between devices, local(): lax.all_to_all(jnp.dot(active, down_weight[0], preferred_element_type=jnp...  161 us
    all_to_all x1, blocking collectives, local(): lax.all_to_all(doubled, ('seq', 'doc'), split_axis=0, concat_axis=0, tile...  143 us
    reduce_scatter x1, waiting for transfers between devices, local(): lax.psum_scatter(jnp.dot(attended, out_weight, preferred_element_type=jnp...  88.8 us
    all_gather x1, waiting for transfers between devices, local(): piece_keys = lax.all_gather(key_heads, 'seq', axis=1, tiled=True)  46.7 us
    unnamed x35, local copies, waits for them, and re-layouts  29.5 us
    dot_general x1, matrix products, local(): jnp.dot(active, down_weight[0], preferred_element_type=jnp.float32)  23.8 us
    all_to_all x1, blocking collectives, local(): lax.all_to_all(jnp.stack(jnp.split(own_out, lax.axis_size('seq'), axis=2)...  18.6 us
    all_gather x1, waiting for transfers between devices, local(): piece_values = lax.all_gather(values, 'seq', axis=1, tiled=True)  15.7 us
  transfers between devices with their start and end apart: 4, of which 4 were waited for; matrix products, arithmetic and copies ran while one was open for 5% of the time, Pallas kernels for 0%

profile of v1, /device:TPU:32, one launch (start us, length us, event | category | flops | bytes accessed | tf_op | source)
XLA Modules:
  0.0 728.0 jit_solution(9340210528176750145)
XLA Ops:
  6.5 0.7 all-gather.3.cloned.1.call-update
  7.3 0.7 all-gather.5.cloned.1.call-update
  8.7 2.3 copy.70
  11.2 46.7 %all-gather.3.cloned.1.call-done = bf16[1,1024,512]{2,1,0:T(8,128)(2,1)} async-done(((bf16[1,128,512]{2,1,0:T(8,128)(2,1)}), bf16[1,1024,512]{2,1,0:T(8,128)(2,1)}) %all-gather.3.cloned.1.call-update) | async-done | bytes 1048592 | tf_op jit(solution)/shard_map/all_gather | solution.py:41
  57.9 2.3 copy.69
  60.1 14.7 %fusion = (f32[8,8,128]{2,1,0:T(8,128)S(1)}, f32[8,1024,128,8]{2,1,3,0:T(8,128)}) fusion(pred[128,1024]{0,1:T(8,128)(4,1)S(1)} %fusion.27, bf16[1024,8,64,1]{0,2,3,1:T(8,128)(2,1)} %bitcast.117, bf16[128,8,8,64]{0,3,2,1:T(8,128)(2,1)} %bitcast.116), kind=kOutput, calls=%fused_computation.5 | convolution fusion | flops 1098899456 | bytes 35815424 | tf_op jit(solution)/shard_map/qkgd,jkd->kgqj/dot_general | solution.py:49
  74.8 14.9 %fusion.1 = f32[8,8,128]{2,1,0:T(8,128)S(1)} fusion(f32[8,1024,128,8]{2,1,3,0:T(8,128)} %get-tuple-element.14, f32[8,8,128]{2,1,0:T(8,128)S(1)} %broadcast_maximum_fusion, pred[128,1024]{0,1:T(8,128)(4,1)S(1)} %fusion.27), kind=kLoop, calls=%fused_computation.6 | loop fusion | flops 41934848 | bytes 33751040 | tf_op jit(solution)/shard_map/reduce_sum | solution.py:55
  89.7 15.7 %all-gather.5.cloned.1.call-done = bf16[1,1024,512]{2,1,0:T(8,128)(2,1)} async-done(((bf16[1,128,512]{2,1,0:T(8,128)(2,1)}), bf16[1,1024,512]{2,1,0:T(8,128)(2,1)}) %all-gather.5.cloned.1.call-update) | async-done | bytes 1048592 | tf_op jit(solution)/shard_map/all_gather | solution.py:42
  105.5 2.3 copy.71
  107.7 14.5 %fusion.18 = bf16[128,8,8,64]{0,3,2,1:T(8,128)(2,1)S(1)} fusion(bf16[1024,8,64,1]{0,2,3,1:T(8,128)(2,1)} %bitcast.119, f32[8,1024,128,8]{2,1,3,0:T(8,128)} %get-tuple-element.14, f32[8,8,128]{2,1,0:T(8,128)S(1)} %broadcast_maximum_fusion, pred[128,1024]{0,1:T(8,128)(4,1)S(1)} %fusion.27, f32[128,8,8]{0,2,1:T(8,128)S(1)} %bitcast.121), kind=kOutput, calls=%fused_computation.28 | convolution fusion | flops 1116733440 | bytes 35848192 | tf_op jit(solution)/shard_map/kgqj,jkd->kgqd/dot_general | solution.py:56
  122.2 0.8 fusion.41
  123.0 1.7 copy.97
  124.7 1.5 bitcast_dynamic-update-slice_fusion.7
  126.2 1.7 copy.98
  127.9 1.7 copy.99
  129.6 1.7 copy.100
  131.2 0.8 copy.101
  132.3 1.6 bitcast_dynamic-update-slice_fusion.6
  133.9 1.6 bitcast_dynamic-update-slice_fusion.5
  135.5 1.6 bitcast_dynamic-update-slice_fusion.4
  137.0 1.6 bitcast_dynamic-update-slice_fusion.3
  139.3 0.7 bitcast_dynamic-update-slice_fusion.1
  139.9 0.7 bitcast_dynamic-update-slice_fusion
  140.6 18.6 %all_to_all.15 = bf16[8,1,128,512]{3,2,1,0:T(8,128)(2,1)S(1)} all-to-all(bf16[8,1,128,512]{3,2,1,0:T(8,128)(2,1)} %bitcast_dynamic-update-slice_fusion), channel_id=1, replica_groups=mesh['seq'=8,'doc'=16] {'seq'}, dimensions={0} | all-to-all | bytes 2097152 | tf_op jit(solution)/shard_map/all_to_all | solution.py:65
  159.2 5.1 convolution_convert_fusion.1
  164.3 8.5 %copy.95 = bf16[1024,2880]{1,0:T(8,128)(2,1)} copy(bf16[1024,2880]{0,1:T(8,128)(2,1)} %convolution_convert_fusion.1) | data formatting | bytes 11796480
  174.3 1.2 reduce-window.6
  176.2 2.4 scatter_custom_fusion
  178.7 88.8 %reduce-scatter.4.cloned.1.call-done = bf16[128,2880]{1,0:T(8,128)(2,1)} async-done(((bf16[1024,2880]{1,0:T(8,128)(2,1)}), bf16[128,2880]{1,0:T(8,128)(2,1)}) %reduce-scatter.4.cloned.1.call-update) | async-done | bytes 737296 | tf_op jit(solution)/shard_map/reduce_scatter | solution.py:68
  267.4 1.3 fusion.25
  269.9 4.8 gather_fusion
  274.8 7.3 %broadcast_in_dim.65 = bf16[64,12,2880]{2,1,0:T(8,128)(2,1)} reshape(bf16[768,2880]{1,0:T(8,128)(2,1)} %gather_fusion) | data formatting | bytes 8847360 | tf_op jit(solution)/shard_map/broadcast_in_dim | solution.py:100
  282.1 4.5 broadcast_in_dim.66
  286.7 143.4 %all_to_all.16 = bf16[128,12,2880]{2,1,0:T(8,128)(2,1)} all-to-all(bf16[128,12,2880]{2,1,0:T(8,128)(2,1)S(1)} %bitcast.115), channel_id=1, replica_groups=mesh['seq'=8,'doc'=16] {'seq','doc'}, dimensions={0} | all-to-all | bytes 17694720 | tf_op jit(solution)/shard_map/all_to_all | solution.py:103
  430.1 14.6 %reshape.106 = bf16[1536,2880]{1,0:T(8,128)(2,1)} reshape(bf16[128,12,2880]{2,1,0:T(8,128)(2,1)} %all_to_all.16) | data formatting | bytes 17694720 | tf_op jit(solution)/shard_map/reshape | solution.py:104
  444.6 12.7 %fusion.8 = f32[1536,768]{1,0:T(8,128)} fusion(bf16[1536,2880]{1,0:T(8,128)(2,1)} %reshape.106, bf16[1,2880,768]{2,1,0:T(8,128)(2,1)} %param.22), kind=kOutput, calls=%fused_computation.18 | convolution fusion | flops 6794772480 | bytes 17989632 | tf_op jit(solution)/shard_map/dot_general | solution.py:106
  457.3 23.8 %convolution_convert_fusion = bf16[1536,2880]{0,1:T(8,128)(2,1)} fusion(bf16[1,768,2880]{1,2,0:T(8,128)(2,1)} %param.23, f32[1536,768]{1,0:T(8,128)} %fusion.8, bf16[1536,2880]{1,0:T(8,128)(2,1)} %reshape.106, bf16[1,2880,768]{2,1,0:T(8,128)(2,1)} %param.21), kind=kOutput, calls=%fused_computation.11 | convolution fusion | flops 13603405824 | bytes 31260672 | tf_op jit(solution)/shard_map/dot_general | solution.py:111
  481.1 12.5 %copy.86 = bf16[1536,2880]{1,0:T(8,128)(2,1)} copy(bf16[1536,2880]{0,1:T(8,128)(2,1)} %convolution_convert_fusion) | data formatting | bytes 17694720 | tf_op jit(solution)/shard_map/convert_element_type | solution.py:112
  493.6 13.5 %reshape.107 = bf16[128,12,2880]{2,1,0:T(8,128)(2,1)} reshape(bf16[1536,2880]{1,0:T(8,128)(2,1)} %copy.86) | data formatting | bytes 17694720 | tf_op jit(solution)/shard_map/reshape | solution.py:113
  507.0 13.9 %all-to-all-start.2 = ((bf16[128,12,2880]{2,1,0:T(8,128)(2,1)}), bf16[128,12,2880]{2,1,0:T(8,128)(2,1)}, u32[]{:S(2)}, u32[]{:S(2)}) async-start(bf16[128,12,2880]{2,1,0:T(8,128)(2,1)} %reshape.107), calls=%async_computation.2 | async-start | bytes 24117248 | tf_op jit(solution)/shard_map/all_to_all | solution.py:110
  521.6 161.0 %all-to-all-done.2 = bf16[128,12,2880]{2,1,0:T(8,128)(2,1)} async-done(((bf16[128,12,2880]{2,1,0:T(8,128)(2,1)}), bf16[128,12,2880]{2,1,0:T(8,128)(2,1)}, u32[]{:S(2)}, u32[]{:S(2)}) %all-to-all-start.2) | async-done | bytes 8847392 | tf_op jit(solution)/shard_map/all_to_all | solution.py:110
  682.5 8.5 %fusion.6 = bf16[64,12,2880]{2,1,0:T(8,128)(2,1)} fusion(bf16[64,2,12,2880]{3,2,1,0:T(8,128)(2,1)} %bitcast.31), kind=kLoop, calls=%fused_computation.12 | loop fusion | flops 8847360 | bytes 13271040 | tf_op jit(solution)/shard_map/convert_element_type | solution.py:16
  691.0 7.9 %reshape.109 = bf16[768,2880]{1,0:T(8,128)(2,1)} reshape(bf16[64,12,2880]{2,1,0:T(8,128)(2,1)} %fusion.6) | data formatting | bytes 8847360 | tf_op jit(solution)/shard_map/reshape | solution.py:123
  698.9 9.6 %gather_fusion.1 = bf16[512,2880]{1,0:T(8,128)(2,1)} fusion(bf16[768,2880]{1,0:T(8,128)(2,1)} %reshape.109, s32[1024]{0:T(1024)S(1)} %get-tuple-element.15), kind=kCustom, calls=%fused_computation.1 | custom fusion | bytes 5900288 | tf_op jit(solution)/shard_map/gather | solution.py:124
  708.6 5.9 reshape.110
  714.5 3.7 fusion.43
  718.2 1.0 fusion.26
  719.2 2.3 copy.89
  (55 shorter events, 5.2 us)
Async XLA Ops:
  6.5 152.7 %copy-start = (bf16[512,2880]{0,1:T(8,128)(2,1)S(1)}, bf16[512,2880]{0,1:T(8,128)(2,1)}, u32[]{:S(2)}) copy-start(bf16[512,2880]{0,1:T(8,128)(2,1)} %param.17) | copy-start | bytes 8847364
  6.5 51.3 %all-gather.3.cloned.1.call-start = ((), (), s32[]{:S(2)}) async-start(), calls=%async_computation.4 | async-start | bytes 1179648 | tf_op jit(solution)/shard_map/all_gather | solution.py:41
  7.3 98.2 %all-gather.5.cloned.1.call-start = ((), (), s32[]{:S(2)}) async-start(), calls=%async_computation.5 | async-start | bytes 1179648 | tf_op jit(solution)/shard_map/all_gather | solution.py:42
  8.0 259.4 %reduce-scatter.4.cloned.1.call-start = ((), (), s32[]{:S(2)}) async-start(), calls=%async_computation.6 | async-start | bytes 6782976 | tf_op jit(solution)/shard_map/reduce_scatter | solution.py:68
  172.8 0.7 copy-start.6
  172.8 1.1 copy-start.4
  172.8 1.5 copy-start.7
  268.7 0.9 copy-start.2
  507.0 13.9 %copy-start.5 = (bf16[2880,64]{0,1:T(8,128)(2,1)S(1)}, bf16[2880,64]{0,1:T(8,128)(2,1)}, u32[]{:S(2)}) copy-start(bf16[2880,64]{0,1:T(8,128)(2,1)} %param.19) | copy-start | bytes 1105924
  507.0 175.5 %all-to-all-start.2 = ((bf16[128,12,2880]{2,1,0:T(8,128)(2,1)}), bf16[128,12,2880]{2,1,0:T(8,128)(2,1)}, u32[]{:S(2)}, u32[]{:S(2)}) async-start(bf16[128,12,2880]{2,1,0:T(8,128)(2,1)} %reshape.107), calls=%async_computation.2 | async-start | bytes 24117248 | tf_op jit(solution)/shard_map/all_to_all | solution.py:110
  708.6 12.9 %copy-start.1 = (bf16[512,2880]{0,1:T(8,128)(2,1)S(1)}, bf16[512,2880]{0,1:T(8,128)(2,1)}, u32[]{:S(2)}) copy-start(bf16[512,2880]{0,1:T(8,128)(2,1)} %param.17) | copy-start | bytes 8847364
  714.5 3.7 copy-start.3
Sparse Core Ops, SparseCore 0:
  9.7 48.1 all-gather.2
  60.2 45.1 all-gather.4
  173.0 94.4 reduce-scatter.3
